TPU v7x, 512 devices: a whole 4x8x8 slice. The times are simulated.
512 devices in a mesh: seq: 16 (over y, core), head: 4 (over x), ivf: 8 (over z).
Axes of the slice: x: 4, y: 8, z: 8, core: 2. Of those that a mesh axis runs over, the one named last changes fastest.
Arguments:
- hidden_in: bfloat16 [8192, 4096], P('seq'), may hold values from -8 to 8
- w_x: bfloat16 [4096, 8192], P('seq', ('head', 'ivf')), may hold values from -0.09375 to 0.09375
- w_z: bfloat16 [4096, 8192], P('seq', ('head', 'ivf')), may hold values from -0.09375 to 0.09375
- w_dt: bfloat16 [4096, 128], P('seq', ('head', 'ivf')), may hold values from -0.09375 to 0.09375
- w_bc: bfloat16 [4096, 2048], P('seq', 'head'), may hold values from -0.0078125 to 0.0078125
- dt_bias: float32 [128], P(('head', 'ivf')), may hold values from -1 to 1
- a_rate: float32 [128], P(('head', 'ivf')), may hold values from 2.4414063e-05 to 0.1
- d_skip: float32 [128], P(('head', 'ivf')), may hold values from 0.5 to 2
- norm_gain: float32 [8192], P(('head', 'ivf')), may hold values from 0.1 to 1.9
- w_out: bfloat16 [8192, 4096], P(('head', 'ivf'), 'seq'), may hold values from -0.0625 to 0.0625
- span_lengths: int32 [32], replicated, may hold values from 1 to 512, 8192 in all
- owners: int32 [32, 1], replicated, may hold values from 0 to 7; in each aligned block of 32 rows (0 to 31, 32 to 63, ...) at most 6 rows name the same one
Outputs:
- ivf_rows: float32 [8, 6, 4096], P('ivf', None, ('seq', 'head'))
Inputs may be any that keep to these rules, and one draw needn't show every extreme that they name: `span_lengths`: the spans cover the slab's tokens in order; the longest has exactly 512 tokens. `owners`: no owner has more than 6 spans, and some owner has exactly 6.
All inputs are finite; a program needn't handle non-finite values.
Results may differ from a plain program's by a relative error of at most 0.0045.
Values may be sent and summed in bfloat16 or wider, within the bound.
A program may use at most 64 MiB of HBM per device.

v0:
```python
import jax
import jax.numpy as jnp
from jax import lax
from jax.sharding import PartitionSpec as P

HEADS = 128
HEAD_DIM = 64
STATE = 128
GROUPS = 8
STRETCH = 128


HIGHEST = lax.Precision.HIGHEST


def entering(part, axis, combine, identity):
    place = lax.axis_index(axis)
    gathered = jax.tree.map(lambda a: lax.all_gather(a, axis), part)
    state = jax.tree.map(lambda a, e: jnp.zeros_like(a) + jnp.asarray(e, a.dtype), part, identity)

    def one(turn, state):
        return combine(
            state, jax.tree.map(lambda a: lax.dynamic_index_in_dim(a, turn, 0, False), gathered)
        )

    return lax.fori_loop(0, place, one, state)


def ssd_blocks(inputs, step_size, log_decay, b_mat, c_mat, block_len):
    length, head_count, head_width = inputs.shape
    group_count, state_dim = (b_mat.shape[1], b_mat.shape[2])
    per_group = head_count // group_count
    block_count = length // block_len

    def split_blocks(source):
        return source.reshape((block_count, block_len) + source.shape[1:])

    blocks = tuple(
        (split_blocks(source) for source in (inputs, step_size, log_decay, b_mat, c_mat))
    )
    lower_tri = jnp.tril(jnp.ones((block_len, block_len), dtype=bool))

    def advance(carried, current):
        block_x, block_dt, block_decay, block_b, block_c = current
        running = jnp.cumsum(block_decay, axis=0)
        head_b = jnp.repeat(block_b, per_group, axis=1)
        head_c = jnp.repeat(block_c, per_group, axis=1)
        scores = jnp.einsum("tgn,sgn->gts", block_c, block_b, precision=HIGHEST)
        scores = jnp.repeat(scores, per_group, axis=0)
        between = running.T[:, :, None] - running.T[:, None, :]
        decays = jnp.where(lower_tri, jnp.exp(jnp.where(lower_tri, between, 0.0)), 0.0)
        weights = scores * decays * block_dt.T[:, None, :]
        within = jnp.einsum("hts,shp->thp", weights, block_x, precision=HIGHEST)
        earlier = jnp.exp(running)[:, :, None] * jnp.einsum(
            "thn,hpn->thp", head_c, carried, precision=HIGHEST
        )
        final_decay = running[-1]
        tail_weight = jnp.exp(final_decay[None, :] - running) * block_dt
        updated = jnp.exp(final_decay)[:, None, None] * carried + jnp.einsum(
            "th,thp,thn->hpn", tail_weight, block_x, head_b, precision=HIGHEST
        )
        return (updated, within + earlier)

    start_state = jnp.zeros((head_count, head_width, state_dim), jnp.float32)
    end_state, outputs = lax.scan(advance, start_state, blocks)
    return (outputs.reshape(length, head_count, head_width), end_state)


def span_average(span_lengths, first_pos, token_count):
    span_ends = jnp.cumsum(span_lengths)
    starts = span_ends - span_lengths
    positions = first_pos + jnp.arange(token_count, dtype=jnp.int32)
    inside = (positions[None, :] >= starts[:, None]) & (positions[None, :] < span_ends[:, None])
    return inside.astype(jnp.float32) / span_lengths[:, None].astype(jnp.float32)


def slot_matrix(owner_ids, owner_count, capacity):
    member = (owner_ids[:, None] == jnp.arange(owner_count, dtype=jnp.int32)[None, :]).astype(
        jnp.int32
    )
    order_in = jnp.sum((jnp.cumsum(member, axis=0) - 1) * member, axis=1)
    slot_ids = owner_ids * capacity + order_in
    return (
        jnp.arange(owner_count * capacity, dtype=jnp.int32)[:, None] == slot_ids[None, :]
    ).astype(jnp.float32)


def local(
    hidden_in, w_x, w_z, w_dt, w_bc, dt_bias, a_rate, d_skip, norm_gain, w_out, span_lengths, owners
):
    seq_count = lax.axis_size("seq")
    head_count = lax.axis_size("head")
    ivf_count = lax.axis_size("ivf")
    seq_index = lax.axis_index("seq")
    head_index = lax.axis_index("head")
    ivf_index = lax.axis_index("ivf")
    tokens = hidden_in.shape[0]
    model_width = hidden_in.shape[1]
    local_heads = w_x.shape[1] // HEAD_DIM
    per_group = HEADS // GROUPS
    pair_cols = 2 * STATE
    local_group = ivf_index * local_heads // per_group
    flat_index = head_index * ivf_count + ivf_index
    bc_weight = lax.dynamic_slice_in_dim(w_bc, local_group * pair_cols, pair_cols, 1)
    pieces = (
        lax.all_gather(w_x, "seq", axis=0, tiled=True),
        lax.all_gather(w_z, "seq", axis=0, tiled=True),
        lax.all_gather(w_dt, "seq", axis=0, tiled=True),
        lax.all_gather(bc_weight, "seq", axis=0, tiled=True),
    )
    x_total, z_total, dt_total, bc_total = tuple(
        (
            jnp.dot(hidden_in, piece_rows, preferred_element_type=jnp.float32)
            for piece_rows in pieces
        )
    )
    inner_x = x_total.astype(jnp.bfloat16)
    gate_z = z_total.astype(jnp.bfloat16)
    bc_own = bc_total.astype(jnp.bfloat16)
    paired = bc_own.astype(jnp.float32).reshape(tokens, 1, 2, STATE)
    b_mat = paired[:, :, 0]
    c_mat = paired[:, :, 1]
    step_size = jax.nn.softplus(dt_total + dt_bias)
    log_decay = -step_size * a_rate
    inputs = inner_x.astype(jnp.float32).reshape(tokens, local_heads, HEAD_DIM)
    scanned, block_state = ssd_blocks(inputs, step_size, log_decay, b_mat, c_mat, STRETCH)
    block_decay = jnp.sum(log_decay, axis=0)

    def compose(earlier, later):
        return (earlier[0] + later[0], jnp.exp(later[0])[:, None, None] * earlier[1] + later[1])

    identity = (jnp.zeros_like(block_decay), jnp.zeros_like(block_state))
    incoming = entering((block_decay, block_state), "seq", compose, identity)
    reach_back = jnp.exp(jnp.cumsum(log_decay, axis=0))
    head_c = jnp.repeat(c_mat, local_heads, axis=1)
    scanned = scanned + reach_back[:, :, None] * jnp.einsum(
        "thn,hpn->thp", head_c, incoming[1], precision=HIGHEST
    )
    with_skip = scanned + d_skip[None, :, None] * inputs
    gated_y = with_skip * jax.nn.silu(gate_z.astype(jnp.float32)).reshape(
        tokens, local_heads, HEAD_DIM
    )
    mean_sq = jnp.sum(gated_y * gated_y, axis=2, keepdims=True) / HEAD_DIM
    normed = (
        (gated_y * lax.rsqrt(mean_sq + 1e-05)).reshape(tokens, local_heads * HEAD_DIM) * norm_gain
    ).astype(jnp.bfloat16)
    averaging = span_average(span_lengths, seq_index * tokens, tokens)
    pooled_y = jnp.dot(averaging, normed.astype(jnp.float32), precision=HIGHEST)
    share_width = model_width // (head_count * ivf_count)
    own_cols = lax.dynamic_slice_in_dim(hidden_in, flat_index * share_width, share_width, 1)
    pooled_u = jnp.dot(averaging, own_cols.astype(jnp.float32), precision=HIGHEST)
    span_count = span_lengths.shape[0]
    capacity = max(2, 3 * span_count // (2 * ivf_count))
    slot_rows = slot_matrix(owners[:, 0], ivf_count, capacity).reshape(
        ivf_count, capacity, span_count
    )
    summed_y, summed_u = lax.psum((pooled_y, pooled_u), "seq")
    block_width = model_width // seq_count
    spread_u = lax.dynamic_update_slice_in_dim(
        jnp.zeros((span_count, model_width), jnp.float32), summed_u, flat_index * share_width, 1
    )
    partial_value = jnp.dot(summed_y, w_out, precision=HIGHEST, preferred_element_type=jnp.float32)
    partial_value = partial_value + lax.dynamic_slice_in_dim(
        spread_u, seq_index * block_width, block_width, 1
    )
    by_block = partial_value.reshape(span_count, head_count, block_width // head_count)
    outbound = jnp.einsum("ocr,rnd->nocd", slot_rows, by_block, precision=HIGHEST)
    received = lax.psum_scatter(
        outbound.reshape(-1, outbound.shape[3]), ("head", "ivf"), scatter_dimension=0, tiled=True
    )
    return received.reshape(1, capacity, received.shape[1])


def solution(mesh):
    return jax.shard_map(
        local,
        mesh=mesh,
        in_specs=(
            P("seq", None),
            P("seq", ("head", "ivf")),
            P("seq", ("head", "ivf")),
            P("seq", ("head", "ivf")),
            P("seq", "head"),
            P(("head", "ivf")),
            P(("head", "ivf")),
            P(("head", "ivf")),
            P(("head", "ivf")),
            P(("head", "ivf"), "seq"),
            P(),
            P(),
        ),
        out_specs=P("ivf", None, ("seq", "head")),
        check_vma=False,
    )
```

profile of v0, /device:TPU:8, one launch (start us, length us, event | category | flops | bytes accessed | tf_op | source)
XLA Modules:
  0.0 398.6 jit_solution(9600328085363465097)
XLA Ops:
  6.5 0.9 copy-done
  8.2 0.7 all-gather.7.cloned.1.call-update
  9.0 0.7 all-gather.11.cloned.1.call-update
  9.7 20.2 %all_gather.24 = bf16[4096,4]{0,1:T(4,128)(2,1)S(1)} all-gather(bf16[256,4]{0,1:T(4,128)(2,1)} %param.19), channel_id=1, replica_groups=mesh['seq'=16,'head'=4,'ivf'=8] {'seq'}, dimensions={0}, use_global_device_ids=true | all-gather | bytes 34816 | tf_op jit(solution)/shard_map/all_gather | solution.py:108
  30.0 3.6 fusion.59
  33.8 21.8 %all-gather.9.cloned.1.call-done = bf16[4096,256]{1,0:T(8,128)(2,1)} async-done(((bf16[256,256]{1,0:T(8,128)(2,1)}), bf16[4096,256]{1,0:T(8,128)(2,1)}) %all-gather.9.cloned.1.call-update) | async-done | bytes 2097168 | tf_op jit(solution)/shard_map/all_gather | solution.py:109
  55.7 4.1 %fusion.31 = f32[256,512]{1,0:T(8,128)S(1)} fusion(bf16[4096,256]{1,0:T(8,128)(2,1)} %all-gather.9.cloned.1.call-done, bf16[512,4096]{1,0:T(8,128)(2,1)} %param.16), kind=kOutput, calls=%fused_computation.46 | convolution fusion | flops 1074003968 | bytes 6815744 | tf_op jit(solution)/shard_map/dot_general | solution.py:113
  60.1 38.6 %all-gather.7.cloned.1.call-done = bf16[4096,256]{1,0:T(8,128)(2,1)} async-done(((bf16[256,256]{1,0:T(8,128)(2,1)}), bf16[4096,256]{1,0:T(8,128)(2,1)}) %all-gather.7.cloned.1.call-update) | async-done | bytes 2097168 | tf_op jit(solution)/shard_map/all_gather | solution.py:106
  98.7 4.2 %fusion.32 = f32[512,256]{0,1:T(8,128)S(1)} fusion(bf16[512,4096]{1,0:T(8,128)(2,1)} %param.16, bf16[4096,256]{1,0:T(8,128)(2,1)} %all-gather.7.cloned.1.call-done), kind=kOutput, calls=%fused_computation.48 | convolution fusion | flops 1074003968 | bytes 6815744 | tf_op jit(solution)/shard_map/dot_general | solution.py:113
  103.1 28.3 %while.27 = (s32[]{:T(128)}, f32[4,64,128]{2,1,0:T(8,128)S(1)}, f32[4,128,4,64]{1,0,3,2:T(4,128)}, f32[4,128,4]{2,1,0:T(8,128)S(1)}, f32[4,128,4]{2,1,0:T(8,128)...) while((s32[]{:T(128)}, f32[4,64,128]{2,1,0:T(8,128)S(1)}, ...), condition=%wide.region_3.4_spmd.clone.clone, body=%wide.region_1.3_spmd.clone.clone.sunk | while | flops 176800256 | bytes 2306288 | solution.py:65
  103.9 0.7 convolution_bitcast_fusion.5
  105.3 4.4 %dynamic_update_slice.12 = f32[4,128,4,64]{1,0,3,2:T(4,128)} dynamic-update-slice(f32[4,128,4,64]{1,0,3,2:T(4,128)} %get-tuple-element.329, f32[1,128,4,64]{1,0,3,2:T(1,128)S(1)} %bitcast.148, s32[]{:T(128)} %get-tuple-element.327, s32[]{:T(128)} %constant.95.clone.1..sunk.1, s32[]{:T(128)} %constant.95.clone.1..sunk.1, s32[]{:T(128)} %constant.95.clone.1..sunk.1) | dynamic-update-slice | bytes 262148 | tf_op jit(solution)/shard_map/while/body/jit(dynamic_update_index_in_dim)/dynamic_update_slice | solution.py:65
  111.0 0.7 convolution_bitcast_fusion.5
  112.4 4.4 %dynamic_update_slice.12 = f32[4,128,4,64]{1,0,3,2:T(4,128)} dynamic-update-slice(f32[4,128,4,64]{1,0,3,2:T(4,128)} %get-tuple-element.329, f32[1,128,4,64]{1,0,3,2:T(1,128)S(1)} %bitcast.148, s32[]{:T(128)} %get-tuple-element.327, s32[]{:T(128)} %constant.95.clone.1..sunk.1, s32[]{:T(128)} %constant.95.clone.1..sunk.1, s32[]{:T(128)} %constant.95.clone.1..sunk.1) | dynamic-update-slice | bytes 262148 | tf_op jit(solution)/shard_map/while/body/jit(dynamic_update_index_in_dim)/dynamic_update_slice | solution.py:65
  118.1 0.7 convolution_bitcast_fusion.5
  119.5 4.4 %dynamic_update_slice.12 = f32[4,128,4,64]{1,0,3,2:T(4,128)} dynamic-update-slice(f32[4,128,4,64]{1,0,3,2:T(4,128)} %get-tuple-element.329, f32[1,128,4,64]{1,0,3,2:T(1,128)S(1)} %bitcast.148, s32[]{:T(128)} %get-tuple-element.327, s32[]{:T(128)} %constant.95.clone.1..sunk.1, s32[]{:T(128)} %constant.95.clone.1..sunk.1, s32[]{:T(128)} %constant.95.clone.1..sunk.1) | dynamic-update-slice | bytes 262148 | tf_op jit(solution)/shard_map/while/body/jit(dynamic_update_index_in_dim)/dynamic_update_slice | solution.py:65
  125.1 0.7 convolution_bitcast_fusion.5
  126.6 4.4 %dynamic_update_slice.12 = f32[4,128,4,64]{1,0,3,2:T(4,128)} dynamic-update-slice(f32[4,128,4,64]{1,0,3,2:T(4,128)} %get-tuple-element.329, f32[1,128,4,64]{1,0,3,2:T(1,128)S(1)} %bitcast.148, s32[]{:T(128)} %get-tuple-element.327, s32[]{:T(128)} %constant.95.clone.1..sunk.1, s32[]{:T(128)} %constant.95.clone.1..sunk.1, s32[]{:T(128)} %constant.95.clone.1..sunk.1) | dynamic-update-slice | bytes 262148 | tf_op jit(solution)/shard_map/while/body/jit(dynamic_update_index_in_dim)/dynamic_update_slice | solution.py:65
  132.1 1.3 dynamic-slice
  134.2 23.0 %all-reduce = f32[64]{0:T(128)S(1)} all-reduce(f32[64]{0:T(128)S(1)} %dynamic-update-slice), channel_id=2, replica_groups=mesh['seq'=16,'head'=4,'ivf'=8] {'seq'}, use_global_device_ids=true, to_apply=%add | all-reduce | flops 64 | bytes 512
  157.5 1.2 reduce-window.19
  159.5 1.3 dynamic-slice.1
  161.7 1.2 fusion.35
  162.8 1.3 reshape.160
  164.2 4.3 %divide_multiply_fusion = f32[512,256]{0,1:T(8,128)S(1)} fusion(bf16[512,4096]{1,0:T(8,128)(2,1)} %param.16, bf16[4096,256]{1,0:T(8,128)(2,1)} %all-gather.11.cloned.1.call-done), kind=kOutput, calls=%fused_computation.55 | convolution fusion | flops 1074528256 | bytes 6815744 | tf_op jit(solution)/shard_map/dot_general | solution.py:113
  168.6 16.3 %all-gather.13.cloned.1.call-done = f32[64,64,128]{2,1,0:T(8,128)} async-done(((f32[4,64,128]{2,1,0:T(8,128)}), f32[64,64,128]{2,1,0:T(8,128)}) %all-gather.13.cloned.1.call-update) | async-done | bytes 2097168 | tf_op jit(solution)/shard_map/all_gather | solution.py:18
  184.9 2.1 while.26
  184.9 1.0 bitcast_add_fusion.2
  185.9 1.0 bitcast_add_fusion.2
  187.0 1.3 multiply_reduce_fusion
  188.8 58.1 %all-reduce.2 = (f32[32,256]{1,0:T(8,128)S(1)}, f32[32,128]{1,0:T(8,128)S(1)}) all-reduce(f32[32,256]{1,0:T(8,128)S(1)} %fusion.38, f32[32,128]{1,0:T(8,128)S(1)} %fusion.35), channel_id=1, replica_groups=mesh['seq'=16,'head'=4,'ivf'=8] {'seq'}, use_global_device_ids=true, to_apply=%region_10.11 | all-reduce | flops 12288 | bytes 98304 | tf_op jit(solution)/shard_map/psum | solution.py:157
  247.6 143.9 %all-reduce.1 = f32[192,64]{1,0:T(8,128)S(1)} all-reduce(f32[192,64]{1,0:T(8,128)S(1)} %reshape.168), channel_id=4, replica_groups=mesh['seq'=16,'head'=4,'ivf'=8] {'head','ivf'}, use_global_device_ids=true, to_apply=%region_14.15.clone | all-reduce | flops 12288 | bytes 98304
  (127 shorter events, 13.3 us)
Async XLA Ops:
  6.5 1.0 copy-start
  6.5 49.1 %all-gather.9.cloned.1.call-start = ((), (), s32[]{:S(2)}) async-start(), calls=%async_computation.1 | async-start | bytes 2228224 | tf_op jit(solution)/shard_map/all_gather | solution.py:109
  8.2 90.5 %all-gather.7.cloned.1.call-start = ((), (), s32[]{:S(2)}) async-start(), calls=%async_computation | async-start | bytes 2228224 | tf_op jit(solution)/shard_map/all_gather | solution.py:106
  8.9 155.3 %all-gather.11.cloned.1.call-start = ((), (), s32[]{:S(2)}) async-start(), calls=%async_computation.2 | async-start | bytes 2228224 | tf_op jit(solution)/shard_map/all_gather | solution.py:107
  9.7 175.2 %all-gather.13.cloned.1.call-start = ((), (), s32[]{:S(2)}) async-start(), calls=%async_computation.3 | async-start | bytes 2228224 | tf_op jit(solution)/shard_map/all_gather | solution.py:18
  103.0 54.3 %copy-start.3 = (f32[4]{0:T(128)S(1)}, f32[4]{0:T(128)}, u32[]{:S(2)}) copy-start(f32[4]{0:T(128)} %param.22) | copy-start | bytes 52
  103.1 56.1 %copy-start.5 = (s32[32]{0:T(128)S(1)}, s32[32]{0:T(128)}, u32[]{:S(2)}) copy-start(s32[32]{0:T(128)} %param.26) | copy-start | bytes 388
  103.1 56.3 %copy-start.4 = (s32[32,1]{0,1:T(1,128)S(1)}, s32[32,1]{0,1:T(1,128)}, u32[]{:S(2)}) copy-start(s32[32,1]{0,1:T(1,128)} %param.27) | copy-start | bytes 388
  131.4 0.6 copy-start.1
  164.2 22.8 %copy-start.7 = (f32[4]{0:T(128)S(1)}, f32[4]{0:T(128)}, u32[]{:S(2)}) copy-start(f32[4]{0:T(128)} %param.23) | copy-start | bytes 52
  168.6 19.8 %copy-start.6 = (f32[256]{0:T(256)S(1)}, f32[256]{0:T(256)}, u32[]{:S(2)}) copy-start(f32[256]{0:T(256)} %param.24) | copy-start | bytes 3076
  168.6 78.4 %copy-start.2 = (bf16[256,256]{1,0:T(8,128)(2,1)S(1)}, bf16[256,256]{1,0:T(8,128)(2,1)}, u32[]{:S(2)}) copy-start(bf16[256,256]{1,0:T(8,128)(2,1)} %param.25) | copy-start | bytes 393220
Sparse Core Ops, SparseCore 0:
  9.5 46.1 all-gather.8
  57.8 40.8 all-gather.6
  100.8 40.8 all-gather.10
  143.7 41.0 all-gather.12
where the time goes:
time: 399 us
  blocking collectives  245 us (61%)
  waiting for transfers between devices  78.1 us (20%)
  local copies, waits for them, and re-layouts  27.8 us (7%)
  matrix products  27.1 us (7%)
  between operations  14.8 us (4%)
  other arithmetic  5.07 us (1%)
    unnamed x2, blocking collectives  167 us
    psum x1, blocking collectives, local(): summed_y, summed_u = lax.psum((pooled_y, pooled_u), 'seq')  58.1 us
    all_gather x1, waiting for transfers between devices, local(): lax.all_gather(w_x, 'seq', axis=0, tiled=True)  38.6 us
    all_gather x1, waiting for transfers between devices, local(): lax.all_gather(bc_weight, 'seq', axis=0, tiled=True)  21.8 us
    all_gather x1, blocking collectives, local(): lax.all_gather(w_dt, 'seq', axis=0, tiled=True)  20.2 us
    dynamic_update_slice x4, local copies, waits for them, and re-layouts, ssd_blocks(): end_state, outputs = lax.scan(advance, start_state, blocks)  17.5 us
    all_gather x1, waiting for transfers between devices, entering(): gathered = jax.tree.map(lambda a: lax.all_gather(a, axis), part)  16.3 us
    dot_general x4, matrix products, local(): jnp.dot(hidden_in, piece_rows, preferred_element_type=jnp.float32)  16.1 us
  transfers between devices with their start and end apart: 4, of which 3 were waited for; matrix products, arithmetic and copies ran while one was open for 13% of the time, Pallas kernels for 0%

commit v1 on v0

v1 whole, which is shorter than its diff:
```python
import jax
import jax.numpy as jnp
from jax import lax
from jax.experimental import pallas as pl
from jax.experimental.pallas import tpu as pltpu
from jax.sharding import PartitionSpec as P

HEADS = 128
HEAD_DIM = 64
STATE = 128
GROUPS = 8
CAP = 6

SEQ = 16
RING = SEQ // 2
NHEAD = 4
NIVF = 8
TOK = 512
KB = 256
CH = 256
LH = CH // HEAD_DIM
SHARE = 4
BCR = 2 * STATE // SHARE
DTR = 16
AR = KB + BCR + DTR
T_CUT = (KB, BCR + DTR, 4, 3)
X_CUTS = ((0, 128, 3, 4), (128, 128, 4, 3))
Z_CUTS = ((0, 128, 3, 4), (128, 128, 4, 3))
SPANS = 32
F32 = jnp.float32
BF16 = jnp.bfloat16
HIGHEST = lax.Precision.HIGHEST
MESH = pl.DeviceIdType.MESH

NN = (((1,), (0,)), ((), ()))
NT = (((1,), (1,)), ((), ()))
TN = (((0,), (0,)), ((), ()))


def dot(a, b, dims=NN, precision=None):
    return lax.dot_general(a, b, dims, precision=precision, preferred_element_type=F32)


def iota(shape, dim):
    return lax.broadcasted_iota(jnp.int32, shape, dim)


def split(v):
    high = v.astype(BF16)
    return high, (v - high.astype(F32)).astype(BF16)


def outward(k, middle):
    return middle + (1 - 2 * (k % 2)) * ((k + 1) // 2)


def lane_sums(v):
    width = v.shape[1]
    lane = iota(v.shape, 1)
    step = 1
    while step < width:
        v = v + jnp.where(lane >= step, pltpu.roll(v, step, 1), 0.0)
        step *= 2
    return v


def kernel(
    hid_hbm, wx_hbm, wz_hbm, wdt_hbm, wbc_hbm, wout_hbm, len_ref, own_ref, bias_ref, rate_ref, skip_ref, gain_ref,
    out_ref,
    hid, abuf, zbuf, xacc, zacc, bacc, bcbuf, wbc, wdt, wout, wpad, pick_slots, ins,
    usrc, urecv, smsg, srecv, sout, sin, scores, cumt, dtt, ybuf, ecum,
    psrc, psib, pall, phalf, fsrc, frecv,
    ld_sem, ring_send, ring_recv, sib_send, sib_recv, bc_send, bc_recv,
    a2a_send, a2a_recv, p_send, p_recv, f_send, f_recv,
):
    seq = lax.axis_index("seq")
    head = lax.axis_index("head")
    ivf = lax.axis_index("ivf")
    y = seq // 2
    c = seq % 2
    up = ((y + 1) % RING) * 2 + c
    down = ((y + RING - 1) % RING) * 2 + c
    sibling = y * 2 + 1 - c
    piece = ivf % SHARE

    def other(k):
        return lax.rem(seq + outward(k, SEQ // 2), SEQ)

    def far(k):
        h = lax.rem(head + outward(k // NIVF, NHEAD // 2), NHEAD)
        o = lax.rem(ivf + outward(k % NIVF, NIVF // 2), NIVF)
        return h, o

    n_seq, n_far = SEQ - 1, NHEAD * NIVF - 1

    lanes = pl.ds(pl.multiple_of((ivf // SHARE) * (2 * STATE) + (piece // 2) * 128, 128), 128)
    loads = [
        pltpu.make_async_copy(wbc_hbm.at[:, lanes], wbc, ld_sem.at[0]),
        pltpu.make_async_copy(wdt_hbm, wdt, ld_sem.at[1]),
        pltpu.make_async_copy(wx_hbm, abuf.at[0, pl.ds(0, KB)], ld_sem.at[2]),
        pltpu.make_async_copy(wz_hbm, zbuf.at[0], ld_sem.at[3]),
        pltpu.make_async_copy(hid_hbm, hid, ld_sem.at[4]),
        pltpu.make_async_copy(wout_hbm, wout, ld_sem.at[5]),
    ]
    for load in loads:
        load.start()

    barrier = pltpu.get_barrier_semaphore()

    def greet_far(k, carry):
        h, o = far(k)
        pl.semaphore_signal(barrier, inc=1, device_id={"head": h, "ivf": o}, device_id_type=MESH)
        return carry

    def greet_seq(k, carry):
        pl.semaphore_signal(barrier, inc=1, device_id={"seq": other(k)}, device_id_type=MESH)
        return carry

    lax.fori_loop(0, n_far, greet_far, 0)
    lax.fori_loop(0, n_seq, greet_seq, 0)

    loads[0].wait()
    loads[1].wait()
    row = iota((BCR, 128), 0) + (piece % 2) * BCR
    take = (row == iota((BCR, 128), 1)).astype(F32).astype(BF16)
    abuf[0, KB : KB + BCR, :] = dot(take, wbc[...], NT).astype(BF16)
    take = (iota((DTR, LH), 0) == iota((DTR, LH), 1)).astype(F32).astype(BF16)
    abuf[0, KB + BCR : AR, :] = dot(take, wdt[...]).astype(BF16)
    xacc[...] = jnp.zeros_like(xacc)
    zacc[...] = jnp.zeros_like(zacc)
    bacc[...] = jnp.zeros_like(bacc)
    loads[2].wait()
    pl.semaphore_wait(barrier, n_seq + n_far)

    cuts = (T_CUT,) + X_CUTS + Z_CUTS

    def ring_ref(n, at):
        buf = abuf if n < 3 else zbuf
        return buf.at[at, pl.ds(cuts[n][0], cuts[n][1])]

    def ring_copy(n, direction, d):
        if direction == 0:
            src, dst, peer = d, d + 1, up
        else:
            src, dst, peer = d + 4 * ((d + 3) // 4), d + 5 - 4 * (d // 3), down
        return pltpu.make_async_remote_copy(
            src_ref=ring_ref(n, src),
            dst_ref=ring_ref(n, dst),
            send_sem=ring_send.at[n, direction, d],
            recv_sem=ring_recv.at[n, dst],
            device_id={"seq": peer},
            device_id_type=MESH,
        )

    def ring_wait(n, at):
        ref = ring_ref(n, at)
        pltpu.make_async_copy(ref, ref, ring_recv.at[n, at]).wait()

    def sib_copy(w, at, part=None):
        buf, sem = (abuf, zbuf)[w], 3 * w
        rows = pl.ds(0, (AR, KB)[w])
        if part == 0:
            rows = pl.ds(0, KB)
        if part == 1:
            rows, sem = pl.ds(KB, AR - KB), 1
        return pltpu.make_async_remote_copy(
            src_ref=buf.at[at, rows],
            dst_ref=buf.at[at + 8, rows],
            send_sem=sib_send.at[sem, at],
            recv_sem=sib_recv.at[sem, at],
            device_id={"seq": sibling},
            device_id_type=MESH,
        )

    def k_block(at):
        m = at % 8
        rel = (m // 5) * (2 * m - 4) - m
        side = at // 8
        core = c + side - 2 * c * side
        return ((y + rel + RING) % RING) * 2 + core

    def hid_cols(at):
        return hid[:, pl.ds(pl.multiple_of(k_block(at) * KB, KB), KB)]

    def mul_t(at):
        bacc[...] += dot(abuf[at, KB:AR, :], hid_cols(at), NT)

    def mul_x(at):
        xacc[...] += dot(hid_cols(at), abuf[at, 0:KB, :])

    def mul_z(at):
        zacc[...] += dot(hid_cols(at), zbuf[at])

    def mul_a(at):
        mul_t(at)
        mul_x(at)

    def two(mul, base):
        def one(i, carry):
            mul(base + 4 * i)
            return carry

        lax.fori_loop(0, 2, one, 0)

    for n in (0, 1, 2):
        ring_copy(n, 0, 0).start()
        ring_copy(n, 1, 0).start()
    sib_copy(0, 0).start()

    lengths = jnp.broadcast_to(len_ref[...].astype(F32), (8, SPANS))
    ends = lengths
    step = 1
    while step < SPANS:
        moved = jnp.concatenate([jnp.zeros((8, step), F32), ends[:, : SPANS - step]], axis=1)
        ends = ends + moved
        step *= 2
    starts = ends - lengths
    member = (jnp.broadcast_to(own_ref[...], (8, SPANS)) == iota((8, SPANS), 0)).astype(F32)
    before = (iota((SPANS, SPANS), 0) < iota((SPANS, SPANS), 1)).astype(F32)
    rank = dot(member, before)
    slot = iota((8, SPANS), 0).astype(F32)
    pos = (iota((8, TOK), 1) + seq * TOK).astype(F32)
    own_first = jnp.zeros((8, 1), F32)
    own_last = jnp.zeros((8, 1), F32)
    for o in range(NIVF):
        chosen = jnp.where(rank[o : o + 1, :] == slot, member[o : o + 1, :], 0.0)
        pick_slots[o * 8 : o * 8 + 8, :] = chosen
        first = jnp.sum(chosen * starts, axis=1, keepdims=True)
        last = jnp.sum(chosen * ends, axis=1, keepdims=True)
        own_first = jnp.where(ivf == o, first, own_first)
        own_last = jnp.where(ivf == o, last, own_last)
    own_ins = ((pos >= own_first) & (pos < own_last)).astype(F32).astype(BF16)
    own_inv = 1.0 / jnp.maximum(own_last - own_first, 1.0)
    span_row = iota((SPANS, SPANS), 0) == iota((SPANS, SPANS), 1)
    span_first = jnp.sum(jnp.where(span_row, starts[0:1, :], 0.0), axis=1, keepdims=True)
    span_last = jnp.sum(jnp.where(span_row, ends[0:1, :], 0.0), axis=1, keepdims=True)
    span_pos = (iota((SPANS, TOK), 1) + seq * TOK).astype(F32)
    ins[...] = ((span_pos >= span_first) & (span_pos < span_last)).astype(F32)
    span_inv = 1.0 / (span_last - span_first)

    loads[4].wait()

    def u_block(s, carry):
        cols = pl.ds(pl.multiple_of(s * KB + (head // 2) * 128, 128), 128)
        usrc[s] = dot(own_ins, hid[:, cols]) * own_inv
        return carry

    lax.fori_loop(0, SEQ, u_block, 0)

    def a2a_start(kind, src_of, dst_of):
        def one(k, carry):
            pltpu.make_async_remote_copy(
                src_ref=src_of(k),
                dst_ref=dst_of(k),
                send_sem=a2a_send.at[kind],
                recv_sem=a2a_recv.at[kind],
                device_id={"seq": other(k)},
                device_id_type=MESH,
            ).start()
            return carry

        lax.fori_loop(0, n_seq, one, 0)

    def a2a_wait(kind, ref):
        pltpu.make_async_copy(ref, ref, a2a_recv.at[kind]).wait()

    def a2a_sent(kind, ref):
        pltpu.make_async_copy(ref, ref, a2a_send.at[kind]).wait()

    a2a_start(0, lambda k: usrc.at[other(k)], lambda k: urecv.at[k])

    mul_a(0)
    sib_copy(0, 0).wait_recv()
    mul_a(8)
    loads[3].wait()

    def a_step(d, carry):
        ring_wait(0, d)
        ring_copy(0, 0, d).start()
        ring_wait(0, 4 + d)

        @pl.when(d < 3)
        def _():
            ring_copy(0, 1, d).start()

        @pl.when(d == 3)
        def _():
            ring_copy(3, 1, 0).start()

        ring_wait(1, 4 + d)
        ring_copy(1, 1, d).start()
        ring_wait(1, d)

        @pl.when(d < 3)
        def _():
            ring_copy(1, 0, d).start()

        @pl.when(d == 3)
        def _():
            ring_copy(4, 0, 0).start()

        ring_wait(2, d)
        ring_copy(2, 0, d).start()
        sib_copy(0, d).start()
        ring_wait(2, 4 + d)

        @pl.when(d < 3)
        def _():
            ring_copy(2, 1, d).start()

        @pl.when(d == 3)
        def _():
            ring_copy(4, 1, 0).start()

        sib_copy(0, 4 + d).start()
        two(mul_a, d)
        sib_copy(0, d).wait_recv()
        sib_copy(0, 4 + d).wait_recv()
        two(mul_a, 8 + d)
        return carry

    lax.fori_loop(1, 4, a_step, 0)
    ring_wait(0, 4)
    sib_copy(0, 4, 1).start()
    ring_copy(3, 0, 0).start()
    sib_copy(1, 0).start()
    mul_t(4)
    sib_copy(0, 4, 1).wait_recv()
    mul_t(12)

    bcbuf[piece] = bacc[0:BCR, :].astype(BF16)

    def bc_copy(j):
        peer = (ivf // SHARE) * SHARE + lax.rem(piece + j, SHARE)
        return pltpu.make_async_remote_copy(
            src_ref=bcbuf.at[piece],
            dst_ref=bcbuf.at[piece],
            send_sem=bc_send,
            recv_sem=bc_recv,
            device_id={"ivf": peer},
            device_id_type=MESH,
        )

    for j in range(1, SHARE):
        bc_copy(j).start()
    ring_wait(1, 4)
    ring_wait(2, 4)
    sib_copy(0, 4, 0).start()
    mul_x(4)

    diag = iota((8, LH), 0) == iota((8, LH), 1)
    bias = jnp.sum(jnp.where(diag, bias_ref[...], 0.0), axis=1, keepdims=True)
    rate = jnp.sum(jnp.where(diag, rate_ref[...], 0.0), axis=1, keepdims=True)
    skip = jnp.sum(jnp.where(diag, skip_ref[...], 0.0), axis=1, keepdims=True)
    raw = bacc[BCR : BCR + 8, :] + bias
    step_size = jnp.maximum(raw, 0.0) + jnp.log1p(jnp.exp(-jnp.abs(raw)))
    cum = lane_sums(-step_size * rate)
    total = cum[:, TOK - 1 : TOK]
    cumt[...] = cum
    dtt[...] = step_size
    spread = (iota((8, CH), 1) // HEAD_DIM == iota((8, CH), 0)).astype(F32)
    tail = dot(jnp.exp(total - cum) * step_size, spread, TN, HIGHEST)
    ecum[...] = dot(jnp.exp(cum), spread, TN, HIGHEST)
    total_row = jnp.sum(total * spread, axis=0, keepdims=True)
    skip_row = jnp.sum(skip * spread, axis=0, keepdims=True)
    sib_copy(0, 4, 0).wait_recv()
    mul_x(12)
    x_b = xacc[...].astype(BF16)
    x_f = x_b.astype(F32)
    w_hi, w_lo = split(x_f * tail)

    pltpu.make_async_copy(bcbuf.at[pl.ds(0, SHARE - 1)], bcbuf.at[pl.ds(0, SHARE - 1)], bc_recv).wait()
    b_t = jnp.concatenate([bcbuf[0], bcbuf[1]], axis=0)
    end_state = (dot(b_t, w_hi) + dot(b_t, w_lo)).astype(BF16)
    d_hi = total_row.astype(BF16)
    left = total_row - d_hi.astype(F32)
    d_mid = left.astype(BF16)
    d_lo = (left - d_mid.astype(F32)).astype(BF16)
    sub16 = iota((16, CH), 0)
    decay_rows = jnp.where(
        sub16 == 0,
        d_hi.astype(F32),
        jnp.where(sub16 == 1, d_mid.astype(F32), jnp.where(sub16 == 2, d_lo.astype(F32), 0.0)),
    ).astype(BF16)
    for s in range(SEQ):
        r, half = s // 2, s % 2
        cols = slice(half * 128, half * 128 + 128)
        smsg[s, 0:16, :] = end_state[r * 16 : r * 16 + 16, cols]
        smsg[s, 16:32, :] = decay_rows[:, cols]
    a2a_start(1, lambda k: smsg.at[other(k)], lambda k: srecv.at[seq])
    srecv[seq] = smsg[seq]

    def z_step(d):
        ring_wait(4, d)
        ring_copy(4, 0, d).start()
        ring_wait(3, 4 + d)
        ring_copy(3, 1, d).start()
        ring_wait(3, d)
        if d < 3:
            ring_copy(3, 0, d).start()
        sib_copy(1, d).start()
        ring_wait(4, 4 + d)
        if d < 3:
            ring_copy(4, 1, d).start()
        sib_copy(1, 4 + d).start()

    def z_use(d):
        two(mul_z, d)
        sib_copy(1, d).wait_recv()
        sib_copy(1, 4 + d).wait_recv()
        two(mul_z, 8 + d)

    z_step(1)
    mul_z(0)
    sib_copy(1, 0).wait_recv()
    mul_z(8)
    c_t = jnp.concatenate([bcbuf[2], bcbuf[3]], axis=0)
    c_m = c_t.astype(F32).T.astype(BF16)
    scores[...] = dot(c_m, b_t)
    ybuf[...] = x_f * skip_row
    z_use(1)

    def one_head(h, carry):
        pick = (iota((8, 128), 0) == h).astype(F32)
        rep = dot(cumt[...], pick, TN, HIGHEST)
        xm = jnp.where(iota((TOK, CH), 1) // HEAD_DIM == h, x_f, 0.0).astype(BF16)
        cum_row = cumt[pl.ds(h, 1), :]
        dt_row = dtt[pl.ds(h, 1), :]
        for i in range(4):
            highs, lows = [], []
            here = slice(i * 128, i * 128 + 128)
            for k in range(i + 1):
                cols = slice(k * 128, k * 128 + 128)
                between = rep[here, :] - cum_row[:, cols]
                if k == i:
                    between = jnp.where(iota((128, 128), 0) >= iota((128, 128), 1), between, -1e30)
                weight = scores[here, cols] * jnp.exp(between) * dt_row[:, cols]
                high, low = split(weight)
                highs.append(high)
                lows.append(low)
            if i:
                highs, lows = [jnp.concatenate(highs, axis=1)], [jnp.concatenate(lows, axis=1)]
            rows = xm[0 : i * 128 + 128, :]
            ybuf[here, :] += dot(highs[0], rows) + dot(lows[0], rows)
        return carry

    lax.fori_loop(0, 2, one_head, 0)
    z_step(2)
    a2a_wait(1, srecv.at[pl.ds(0, n_seq)])

    def enter(s, carried):
        sout[s] = carried.astype(BF16)
        block = srecv[s].astype(F32)
        decay = jnp.exp(block[16:17, :] + block[17:18, :] + block[18:19, :])
        return decay * carried + block[0:16, :]

    lax.fori_loop(0, SEQ, enter, jnp.zeros((16, 128), F32))
    a2a_start(2, lambda k: sout.at[other(k)], lambda k: sin.at[seq])
    sin[seq] = sout[seq]
    z_use(2)
    lax.fori_loop(2, 4, one_head, 0)

    z_step(3)
    z_use(3)
    loads[5].wait()
    at_col = iota((CH, NHEAD * 128), 1)
    wanted = (at_col // 128) * 64 + at_col % 128
    take = (at_col % 128 < 64) & (wanted == iota((CH, NHEAD * 128), 0))
    wpad[...] = dot(wout[...], take.astype(F32).astype(BF16)).astype(BF16)
    ring_wait(3, 4)
    ring_wait(4, 4)
    sib_copy(1, 4).start()
    mul_z(4)
    sib_copy(1, 4).wait_recv()
    mul_z(12)
    z = zacc[...].astype(BF16).astype(F32)
    gate = z / (1.0 + jnp.exp(-z))

    a2a_wait(2, sin.at[pl.ds(0, n_seq)])
    entering = jnp.concatenate(
        [jnp.concatenate([sin[2 * r], sin[2 * r + 1]], axis=1) for r in range(8)], axis=0
    )
    gated = (ybuf[...] + ecum[...] * dot(c_m, entering)) * gate
    sq_hi, sq_lo = split(gated * gated)
    same = (iota((CH, CH), 0) // HEAD_DIM == iota((CH, CH), 1) // HEAD_DIM).astype(F32).astype(BF16)
    mean_sq = (dot(sq_hi, same) + dot(sq_lo, same)) * (1.0 / HEAD_DIM)
    normed = (gated * lax.rsqrt(mean_sq + 1e-05) * gain_ref[...]).astype(BF16)
    pooled = dot(ins[...].astype(BF16), normed) * span_inv
    psrc[0] = pooled[:, 0:128]
    psrc[1] = pooled[:, 128:256]

    def to_sibling(kind, src, dst):
        return pltpu.make_async_remote_copy(
            src_ref=src,
            dst_ref=dst,
            send_sem=p_send.at[kind],
            recv_sem=p_recv.at[kind],
            device_id={"seq": sibling},
            device_id_type=MESH,
        )

    first_half = to_sibling(0, psrc.at[1 - c], psib)
    first_half.start()
    first_half.wait_recv()
    pall[y] = psrc[c] + psib[...]

    def p_start(k, carry):
        peer = lax.rem(y + outward(k, RING // 2), RING) * 2 + c
        pltpu.make_async_remote_copy(
            src_ref=pall.at[y],
            dst_ref=pall.at[y],
            send_sem=p_send.at[1],
            recv_sem=p_recv.at[1],
            device_id={"seq": peer},
            device_id_type=MESH,
        ).start()
        return carry

    lax.fori_loop(0, RING - 1, p_start, 0)
    most = pall.at[pl.ds(0, RING - 1)]
    pltpu.make_async_copy(most, most, p_recv.at[1]).wait()
    phalf[c] = jnp.sum(pall[...], axis=0)
    second_half = to_sibling(2, phalf.at[c], phalf.at[c])
    second_half.start()
    second_half.wait_recv()
    s_hi, s_lo = split(jnp.concatenate([phalf[0], phalf[1]], axis=1))
    slots = pick_slots[...].astype(BF16)
    value = dot(dot(slots, s_hi).astype(BF16), wpad[...]) + dot(
        dot(slots, s_lo).astype(BF16), wpad[...]
    )
    for o in range(NIVF):
        for h in range(NHEAD):
            fsrc[h * NIVF + o] = value[o * 8 : o * 8 + 8, h * 128 : h * 128 + 128]

    def f_start(k, carry):
        h, o = far(k)
        pltpu.make_async_remote_copy(
            src_ref=fsrc.at[h * NIVF + o],
            dst_ref=frecv.at[k],
            send_sem=f_send,
            recv_sem=f_recv,
            device_id={"head": h, "ivf": o},
            device_id_type=MESH,
        ).start()
        return carry

    lax.fori_loop(0, n_far, f_start, 0)

    def sent(d, carry):
        for n in range(5):
            for direction in (0, 1):
                if cuts[n][2 + direction] == 4:
                    ring_copy(n, direction, d).wait_send()
                else:

                    @pl.when(d < 3)
                    def _():
                        ring_copy(n, direction, d).wait_send()

        return carry

    def sib_sent(at, carry):
        @pl.when(at != 4)
        def _():
            sib_copy(0, at).wait_send()

        sib_copy(1, at).wait_send()
        return carry

    lax.fori_loop(0, 4, sent, 0)
    lax.fori_loop(0, 8, sib_sent, 0)
    sib_copy(0, 4, 0).wait_send()
    sib_copy(0, 4, 1).wait_send()
    pltpu.make_async_copy(bcbuf.at[pl.ds(0, SHARE - 1)], bcbuf.at[pl.ds(0, SHARE - 1)], bc_send).wait()
    a2a_sent(0, urecv)
    a2a_sent(1, srecv.at[pl.ds(0, n_seq)])
    a2a_sent(2, sin.at[pl.ds(0, n_seq)])
    first_half.wait_send()
    second_half.wait_send()
    pltpu.make_async_copy(most, most, p_send.at[1]).wait()

    a2a_wait(0, urecv)
    mean_u = usrc[seq] + jnp.sum(urecv[...], axis=0)
    mean_u = jnp.where(head % 2 == 0, mean_u[:, 0:64], mean_u[:, 64:128])
    own = fsrc[head * NIVF + ivf]
    pltpu.make_async_copy(frecv, frecv, f_recv).wait()
    result = (own + jnp.sum(frecv[...], axis=0))[:, 0:64] + mean_u
    out_ref[0] = result[0:CAP, :]
    pltpu.make_async_copy(frecv, frecv, f_send).wait()


def local(
    hidden_in, w_x, w_z, w_dt, w_bc, dt_bias, a_rate, d_skip, norm_gain, w_out, span_lengths, owners
):
    any_spec = pl.BlockSpec(memory_space=pl.ANY)
    vmem_spec = pl.BlockSpec(memory_space=pltpu.VMEM)
    vmem = pltpu.VMEM
    dma = pltpu.SemaphoreType.DMA
    return pl.pallas_call(
        kernel,
        out_shape=jax.ShapeDtypeStruct((1, CAP, 64), F32),
        in_specs=[any_spec] * 6 + [vmem_spec] * 6,
        out_specs=vmem_spec,
        scratch_shapes=[
            vmem((TOK, SEQ * KB), BF16),
            vmem((SEQ, AR, CH), BF16),
            vmem((SEQ, KB, CH), BF16),
            vmem((TOK, CH), F32),
            vmem((TOK, CH), F32),
            vmem((BCR + DTR, TOK), F32),
            vmem((SHARE, BCR, TOK), BF16),
            vmem((KB, 128), BF16),
            vmem((LH, KB), BF16),
            vmem((CH, 256), BF16),
            vmem((CH, NHEAD * 128), BF16),
            vmem((64, SPANS), F32),
            vmem((SPANS, TOK), F32),
            vmem((SEQ, 8, 128), F32),
            vmem((SEQ - 1, 8, 128), F32),
            vmem((SEQ, 32, 128), BF16),
            vmem((SEQ, 32, 128), BF16),
            vmem((SEQ, 16, 128), BF16),
            vmem((SEQ, 16, 128), BF16),
            vmem((TOK, TOK), F32),
            vmem((8, TOK), F32),
            vmem((8, TOK), F32),
            vmem((TOK, CH), F32),
            vmem((TOK, CH), F32),
            vmem((2, SPANS, 128), F32),
            vmem((SPANS, 128), F32),
            vmem((RING, SPANS, 128), F32),
            vmem((2, SPANS, 128), F32),
            vmem((NHEAD * NIVF, 8, 128), F32),
            vmem((NHEAD * NIVF - 1, 8, 128), F32),
            dma((6,)),
            dma((5, 2, 4)),
            dma((5, 8)),
            dma((4, 8)),
            dma((4, 8)),
            dma,
            dma,
            dma((3,)),
            dma((3,)),
            dma((3,)),
            dma((3,)),
            dma,
            dma,
        ],
        compiler_params=pltpu.CompilerParams(
            collective_id=0, has_side_effects=True, vmem_limit_bytes=64 * 1024 * 1024
        ),
    )(
        hidden_in,
        w_x,
        w_z,
        w_dt.T,
        w_bc,
        w_out,
        span_lengths.reshape(1, SPANS),
        owners.T,
        dt_bias.reshape(1, LH),
        a_rate.reshape(1, LH),
        d_skip.reshape(1, LH),
        norm_gain.reshape(1, CH),
    )


def solution(mesh):
    return jax.shard_map(
        local,
        mesh=mesh,
        in_specs=(
            P("seq", None),
            P("seq", ("head", "ivf")),
            P("seq", ("head", "ivf")),
            P("seq", ("head", "ivf")),
            P("seq", "head"),
            P(("head", "ivf")),
            P(("head", "ivf")),
            P(("head", "ivf")),
            P(("head", "ivf")),
            P(("head", "ivf"), "seq"),
            P(),
            P(),
        ),
        out_specs=P("ivf", None, ("seq", "head")),
        check_vma=False,
    )
```

time: 399 us -> 76.3 us (0.19)
  the two profiles are of different devices: /device:TPU:8 before, /device:TPU:1 now
where the time goes in v1:
time: 76.3 us; the launch traced here: 76.1 us
  Pallas kernels  74.9 us (98%)
  local copies, waits for them, and re-layouts  1.26 us (2%)
    pallas_call x1, Pallas kernels, local(): pl.pallas_call(kernel, out_shape=jax.ShapeDtypeStruct((1, CAP, 64), F32),...  74.9 us

profile of v1, /device:TPU:1, one launch (start us, length us, event | category | flops | bytes accessed | tf_op | source)
XLA Modules:
  0.0 76.1 jit_solution(16153722487074087887)
XLA Ops:
  0.0 74.9 %shard_map.118 = f32[1,6,64]{2,1,0:T(8,128)} custom-call(bf16[512,4096]{1,0:T(8,128)(2,1)} %hid_hbm.1, bf16[256,256]{1,0:T(8,128)(2,1)} %wx_hbm.1, bf16[256,256]{1,0:T(8,128)(2,1)} %wz_hbm.1, bf16[4,256]{1,0:T(4,128)(2,1)} %bitcast.7, bf16[256,512]{1,0:T(8,128)(2,1)} %wbc_hbm.1, bf16[256,256]{1,0:T(8,128)(2,1)} %wout_hbm.1, s32[1,32]{1,0:T(1,128)} %bitcast.9, ...), custom_call_target="tpu_custom_call" | custom-call | tf_op jit(solution)/shard_map/pallas_call | solution.py:599
  74.9 1.3 %copy.13 = f32[1,6,64]{2,0,1:T(1,128)} copy(f32[1,6,64]{2,1,0:T(8,128)} %shard_map.118) | data formatting | bytes 3072 | tf_op jit(solution)/shard_map/pallas_call | solution.py:599

commit v2 on v1

--- a/solution.py
+++ b/solution.py
@@ -21,6 +21,7 @@
 LH = CH // HEAD_DIM
 SHARE = 4
 BCR = 2 * STATE // SHARE
+HALF = BCR // 2
 DTR = 16
 AR = KB + BCR + DTR
 T_CUT = (KB, BCR + DTR, 4, 3)
@@ -65,10 +66,12 @@
 
 
 def kernel(
-    hid_hbm, wx_hbm, wz_hbm, wdt_hbm, wbc_hbm, wout_hbm, len_ref, own_ref, bias_ref, rate_ref, skip_ref, gain_ref,
+    hid_hbm, wx_hbm, wz_hbm, wdt_hbm, wbc_hbm, wout_hbm,
+    len_hbm, own_hbm, bias_hbm, rate_hbm, skip_hbm, gain_hbm,
     out_ref,
+    len_ref, own_ref, bias_ref, rate_ref, skip_ref, gain_ref,
     hid, abuf, zbuf, xacc, zacc, bacc, bcbuf, wbc, wdt, wout, wpad, pick_slots, ins,
-    usrc, urecv, smsg, srecv, sout, sin, scores, cumt, dtt, ybuf, ecum,
+    usrc, urecv, dmsg, drecv, smsg, srecv, sout, sin, scores, cumt, dtt, ybuf, ecum,
     psrc, psib, pall, phalf, fsrc, frecv,
     ld_sem, ring_send, ring_recv, sib_send, sib_recv, bc_send, bc_recv,
     a2a_send, a2a_recv, p_send, p_recv, f_send, f_recv,
@@ -93,7 +96,7 @@
 
     n_seq, n_far = SEQ - 1, NHEAD * NIVF - 1
 
-    lanes = pl.ds(pl.multiple_of((ivf // SHARE) * (2 * STATE) + (piece // 2) * 128, 128), 128)
+    lanes = pl.ds(pl.multiple_of((ivf // SHARE) * (2 * STATE), 2 * STATE), 2 * STATE)
     loads = [
         pltpu.make_async_copy(wbc_hbm.at[:, lanes], wbc, ld_sem.at[0]),
         pltpu.make_async_copy(wdt_hbm, wdt, ld_sem.at[1]),
@@ -101,10 +104,13 @@
         pltpu.make_async_copy(wz_hbm, zbuf.at[0], ld_sem.at[3]),
         pltpu.make_async_copy(hid_hbm, hid, ld_sem.at[4]),
         pltpu.make_async_copy(wout_hbm, wout, ld_sem.at[5]),
+        pltpu.make_async_copy(len_hbm, len_ref, ld_sem.at[6]),
+        pltpu.make_async_copy(own_hbm, own_ref, ld_sem.at[7]),
+        pltpu.make_async_copy(bias_hbm, bias_ref, ld_sem.at[8]),
+        pltpu.make_async_copy(rate_hbm, rate_ref, ld_sem.at[9]),
+        pltpu.make_async_copy(skip_hbm, skip_ref, ld_sem.at[10]),
+        pltpu.make_async_copy(gain_hbm, gain_ref, ld_sem.at[11]),
     ]
-    for load in loads:
-        load.start()
-
     barrier = pltpu.get_barrier_semaphore()
 
     def greet_far(k, carry):
@@ -118,17 +124,17 @@
 
     lax.fori_loop(0, n_far, greet_far, 0)
     lax.fori_loop(0, n_seq, greet_seq, 0)
+    for load in loads:
+        load.start()
 
     loads[0].wait()
     loads[1].wait()
-    row = iota((BCR, 128), 0) + (piece % 2) * BCR
-    take = (row == iota((BCR, 128), 1)).astype(F32).astype(BF16)
+    row = iota((BCR, 2 * STATE), 0)
+    row = row + (row // HALF) * (STATE - HALF) + piece * HALF
+    take = (row == iota((BCR, 2 * STATE), 1)).astype(F32).astype(BF16)
     abuf[0, KB : KB + BCR, :] = dot(take, wbc[...], NT).astype(BF16)
     take = (iota((DTR, LH), 0) == iota((DTR, LH), 1)).astype(F32).astype(BF16)
     abuf[0, KB + BCR : AR, :] = dot(take, wdt[...]).astype(BF16)
-    xacc[...] = jnp.zeros_like(xacc)
-    zacc[...] = jnp.zeros_like(zacc)
-    bacc[...] = jnp.zeros_like(bacc)
     loads[2].wait()
     pl.semaphore_wait(barrier, n_seq + n_far)
 
@@ -156,18 +162,14 @@
         ref = ring_ref(n, at)
         pltpu.make_async_copy(ref, ref, ring_recv.at[n, at]).wait()
 
-    def sib_copy(w, at, part=None):
-        buf, sem = (abuf, zbuf)[w], 3 * w
-        rows = pl.ds(0, (AR, KB)[w])
-        if part == 0:
-            rows = pl.ds(0, KB)
-        if part == 1:
-            rows, sem = pl.ds(KB, AR - KB), 1
+    def sib_copy(kind, at):
+        buf = (abuf, abuf, zbuf)[kind]
+        rows = (pl.ds(0, KB), pl.ds(KB, AR - KB), pl.ds(0, KB))[kind]
         return pltpu.make_async_remote_copy(
             src_ref=buf.at[at, rows],
             dst_ref=buf.at[at + 8, rows],
-            send_sem=sib_send.at[sem, at],
-            recv_sem=sib_recv.at[sem, at],
+            send_sem=sib_send.at[kind, at],
+            recv_sem=sib_recv.at[kind, at],
             device_id={"seq": sibling},
             device_id_type=MESH,
         )
@@ -191,22 +193,34 @@
     def mul_z(at):
         zacc[...] += dot(hid_cols(at), zbuf[at])
 
-    def mul_a(at):
-        mul_t(at)
-        mul_x(at)
-
-    def two(mul, base):
+    muls = (mul_x, mul_t, mul_z)
+
+    def use_mine(kind, d, count):
         def one(i, carry):
-            mul(base + 4 * i)
+            muls[kind](d + 4 * i)
             return carry
 
-        lax.fori_loop(0, 2, one, 0)
+        lax.fori_loop(0, count, one, 0)
+
+    def use_sib(kind, d, count):
+        def one(i, carry):
+            sib_copy(kind, d + 4 * i).wait_recv()
+            muls[kind](8 + d + 4 * i)
+            return carry
+
+        lax.fori_loop(0, count, one, 0)
 
     for n in (0, 1, 2):
         ring_copy(n, 0, 0).start()
         ring_copy(n, 1, 0).start()
+    sib_copy(1, 0).start()
     sib_copy(0, 0).start()
-
+    xacc[...] = jnp.zeros_like(xacc)
+    zacc[...] = jnp.zeros_like(zacc)
+    bacc[...] = jnp.zeros_like(bacc)
+
+    for load in loads[6:]:
+        load.wait()
     lengths = jnp.broadcast_to(len_ref[...].astype(F32), (8, SPANS))
     ends = lengths
     step = 1
@@ -238,17 +252,8 @@
     ins[...] = ((span_pos >= span_first) & (span_pos < span_last)).astype(F32)
     span_inv = 1.0 / (span_last - span_first)
 
-    loads[4].wait()
-
-    def u_block(s, carry):
-        cols = pl.ds(pl.multiple_of(s * KB + (head // 2) * 128, 128), 128)
-        usrc[s] = dot(own_ins, hid[:, cols]) * own_inv
-        return carry
-
-    lax.fori_loop(0, SEQ, u_block, 0)
-
     def a2a_start(kind, src_of, dst_of):
-        def one(k, carry):
+        for k in range(n_seq):
             pltpu.make_async_remote_copy(
                 src_ref=src_of(k),
                 dst_ref=dst_of(k),
@@ -257,9 +262,6 @@
                 device_id={"seq": other(k)},
                 device_id_type=MESH,
             ).start()
-            return carry
-
-        lax.fori_loop(0, n_seq, one, 0)
 
     def a2a_wait(kind, ref):
         pltpu.make_async_copy(ref, ref, a2a_recv.at[kind]).wait()
@@ -267,14 +269,33 @@
     def a2a_sent(kind, ref):
         pltpu.make_async_copy(ref, ref, a2a_send.at[kind]).wait()
 
-    a2a_start(0, lambda k: usrc.at[other(k)], lambda k: urecv.at[k])
-
-    mul_a(0)
-    sib_copy(0, 0).wait_recv()
-    mul_a(8)
     loads[3].wait()
+    loads[4].wait()
+    def u_block(s, carry):
+        cols = pl.ds(pl.multiple_of(s * KB + (head // 2) * 128, 128), 128)
+        usrc[s] = dot(own_ins, hid[:, cols]) * own_inv
+        return carry
+
+    lax.fori_loop(0, SEQ, u_block, 0)
+
+
+    def z_start(n):
+        ring_copy(n, 0, 0).start()
+        ring_copy(n, 1, 0).start()
+
+    def z_step(n, d):
+        ring_wait(n, d)
+        if d < cuts[n][2]:
+            ring_copy(n, 0, d).start()
+        ring_wait(n, 4 + d)
+        if d < cuts[n][3]:
+            ring_copy(n, 1, d).start()
+        if n == 4:
+            sib_copy(2, d).start()
+            sib_copy(2, 4 + d).start()
 
     def a_step(d, carry):
+        before = 1 + (d + 1) // 3
         ring_wait(0, d)
         ring_copy(0, 0, d).start()
         ring_wait(0, 4 + d)
@@ -283,10 +304,10 @@
         def _():
             ring_copy(0, 1, d).start()
 
-        @pl.when(d == 3)
-        def _():
-            ring_copy(3, 1, 0).start()
-
+        sib_copy(1, d).start()
+        sib_copy(1, 4 + d).start()
+        use_mine(1, d - 1, before)
+        use_mine(0, d - 1, before)
         ring_wait(1, 4 + d)
         ring_copy(1, 1, d).start()
         ring_wait(1, d)
@@ -295,58 +316,59 @@
         def _():
             ring_copy(1, 0, d).start()
 
-        @pl.when(d == 3)
-        def _():
-            ring_copy(4, 0, 0).start()
-
+        use_sib(1, d - 1, before)
+        use_sib(0, d - 1, before)
         ring_wait(2, d)
         ring_copy(2, 0, d).start()
-        sib_copy(0, d).start()
         ring_wait(2, 4 + d)
 
         @pl.when(d < 3)
         def _():
             ring_copy(2, 1, d).start()
 
+        sib_copy(0, d).start()
+        sib_copy(0, 4 + d).start()
+
+        @pl.when(d == 2)
+        def _():
+            z_start(3)
+            z_start(4)
+
         @pl.when(d == 3)
         def _():
-            ring_copy(4, 1, 0).start()
-
-        sib_copy(0, 4 + d).start()
-        two(mul_a, d)
-        sib_copy(0, d).wait_recv()
-        sib_copy(0, 4 + d).wait_recv()
-        two(mul_a, 8 + d)
+            z_step(3, 1)
+            z_step(4, 1)
+
         return carry
 
     lax.fori_loop(1, 4, a_step, 0)
     ring_wait(0, 4)
-    sib_copy(0, 4, 1).start()
-    ring_copy(3, 0, 0).start()
-    sib_copy(1, 0).start()
+    sib_copy(1, 4).start()
+    use_mine(1, 3, 2)
+    use_sib(1, 3, 2)
     mul_t(4)
-    sib_copy(0, 4, 1).wait_recv()
-    mul_t(12)
-
-    bcbuf[piece] = bacc[0:BCR, :].astype(BF16)
-
-    def bc_copy(j):
+    use_sib(1, 4, 1)
+
+    for part in (0, 1):
+        bcbuf[part, piece] = bacc[part * HALF : part * HALF + HALF, :].astype(BF16)
+
+    def bc_copy(part, j):
         peer = (ivf // SHARE) * SHARE + lax.rem(piece + j, SHARE)
         return pltpu.make_async_remote_copy(
-            src_ref=bcbuf.at[piece],
-            dst_ref=bcbuf.at[piece],
-            send_sem=bc_send,
-            recv_sem=bc_recv,
+            src_ref=bcbuf.at[part, piece],
+            dst_ref=bcbuf.at[part, piece],
+            send_sem=bc_send.at[part],
+            recv_sem=bc_recv.at[part],
             device_id={"ivf": peer},
             device_id_type=MESH,
         )
 
-    for j in range(1, SHARE):
-        bc_copy(j).start()
-    ring_wait(1, 4)
-    ring_wait(2, 4)
-    sib_copy(0, 4, 0).start()
-    mul_x(4)
+    def bc_wait(part, sem):
+        ref = bcbuf.at[part, pl.ds(0, SHARE - 1)]
+        pltpu.make_async_copy(ref, ref, sem.at[part]).wait()
+
+    for j in (2, 1, 3):
+        bc_copy(0, j).start()
 
     diag = iota((8, LH), 0) == iota((8, LH), 1)
     bias = jnp.sum(jnp.where(diag, bias_ref[...], 0.0), axis=1, keepdims=True)
@@ -363,62 +385,43 @@
     ecum[...] = dot(jnp.exp(cum), spread, TN, HIGHEST)
     total_row = jnp.sum(total * spread, axis=0, keepdims=True)
     skip_row = jnp.sum(skip * spread, axis=0, keepdims=True)
-    sib_copy(0, 4, 0).wait_recv()
-    mul_x(12)
+    for half in (0, 1):
+        dmsg[half] = jnp.broadcast_to(total_row[:, half * 128 : half * 128 + 128], (8, 128))
+    a2a_start(3, lambda k: dmsg.at[other(k) % 2], lambda k: drecv.at[seq])
+    drecv[seq] = dmsg[c]
+    use_mine(0, 3, 2)
+    use_sib(0, 3, 2)
+    ring_wait(1, 4)
+    ring_wait(2, 4)
+    sib_copy(0, 4).start()
+    z_step(3, 2)
+    z_step(4, 2)
+    sib_copy(2, 0).start()
+    mul_x(4)
+
+    use_sib(0, 4, 1)
     x_b = xacc[...].astype(BF16)
     x_f = x_b.astype(F32)
     w_hi, w_lo = split(x_f * tail)
 
-    pltpu.make_async_copy(bcbuf.at[pl.ds(0, SHARE - 1)], bcbuf.at[pl.ds(0, SHARE - 1)], bc_recv).wait()
-    b_t = jnp.concatenate([bcbuf[0], bcbuf[1]], axis=0)
-    end_state = (dot(b_t, w_hi) + dot(b_t, w_lo)).astype(BF16)
-    d_hi = total_row.astype(BF16)
-    left = total_row - d_hi.astype(F32)
-    d_mid = left.astype(BF16)
-    d_lo = (left - d_mid.astype(F32)).astype(BF16)
-    sub16 = iota((16, CH), 0)
-    decay_rows = jnp.where(
-        sub16 == 0,
-        d_hi.astype(F32),
-        jnp.where(sub16 == 1, d_mid.astype(F32), jnp.where(sub16 == 2, d_lo.astype(F32), 0.0)),
-    ).astype(BF16)
+    bc_wait(0, bc_recv)
+    b_t = bcbuf[0].reshape(STATE, TOK)
+    end_state = dot(b_t, w_hi) + dot(b_t, w_lo)
     for s in range(SEQ):
         r, half = s // 2, s % 2
         cols = slice(half * 128, half * 128 + 128)
-        smsg[s, 0:16, :] = end_state[r * 16 : r * 16 + 16, cols]
-        smsg[s, 16:32, :] = decay_rows[:, cols]
+        smsg[s] = end_state[r * 16 : r * 16 + 16, cols]
     a2a_start(1, lambda k: smsg.at[other(k)], lambda k: srecv.at[seq])
     srecv[seq] = smsg[seq]
 
-    def z_step(d):
-        ring_wait(4, d)
-        ring_copy(4, 0, d).start()
-        ring_wait(3, 4 + d)
-        ring_copy(3, 1, d).start()
-        ring_wait(3, d)
-        if d < 3:
-            ring_copy(3, 0, d).start()
-        sib_copy(1, d).start()
-        ring_wait(4, 4 + d)
-        if d < 3:
-            ring_copy(4, 1, d).start()
-        sib_copy(1, 4 + d).start()
-
-    def z_use(d):
-        two(mul_z, d)
-        sib_copy(1, d).wait_recv()
-        sib_copy(1, 4 + d).wait_recv()
-        two(mul_z, 8 + d)
-
-    z_step(1)
-    mul_z(0)
-    sib_copy(1, 0).wait_recv()
-    mul_z(8)
-    c_t = jnp.concatenate([bcbuf[2], bcbuf[3]], axis=0)
-    c_m = c_t.astype(F32).T.astype(BF16)
+    for j in (2, 1, 3):
+        bc_copy(1, j).start()
+    z_step(3, 3)
+    z_step(4, 3)
+    bc_wait(1, bc_recv)
+    c_m = bcbuf[1].reshape(STATE, TOK).astype(F32).T.astype(BF16)
     scores[...] = dot(c_m, b_t)
     ybuf[...] = x_f * skip_row
-    z_use(1)
 
     def one_head(h, carry):
         pick = (iota((8, 128), 0) == h).astype(F32)
@@ -444,24 +447,24 @@
             ybuf[here, :] += dot(highs[0], rows) + dot(lows[0], rows)
         return carry
 
-    lax.fori_loop(0, 2, one_head, 0)
-    z_step(2)
+    lax.fori_loop(0, LH, one_head, 0)
+    a2a_wait(3, drecv.at[pl.ds(0, n_seq)])
     a2a_wait(1, srecv.at[pl.ds(0, n_seq)])
 
     def enter(s, carried):
-        sout[s] = carried.astype(BF16)
-        block = srecv[s].astype(F32)
-        decay = jnp.exp(block[16:17, :] + block[17:18, :] + block[18:19, :])
-        return decay * carried + block[0:16, :]
+        sout[s] = carried
+        return jnp.exp(drecv[s][0:1, :]) * carried + srecv[s]
 
     lax.fori_loop(0, SEQ, enter, jnp.zeros((16, 128), F32))
     a2a_start(2, lambda k: sout.at[other(k)], lambda k: sin.at[seq])
     sin[seq] = sout[seq]
-    z_use(2)
-    lax.fori_loop(2, 4, one_head, 0)
-
-    z_step(3)
-    z_use(3)
+    mul_z(0)
+    use_sib(2, 0, 1)
+    use_mine(2, 1, 2)
+    use_sib(2, 1, 2)
+
+    use_mine(2, 2, 2)
+    use_sib(2, 2, 2)
     loads[5].wait()
     at_col = iota((CH, NHEAD * 128), 1)
     wanted = (at_col // 128) * 64 + at_col % 128
@@ -469,18 +472,21 @@
     wpad[...] = dot(wout[...], take.astype(F32).astype(BF16)).astype(BF16)
     ring_wait(3, 4)
     ring_wait(4, 4)
-    sib_copy(1, 4).start()
+    sib_copy(2, 4).start()
+    use_mine(2, 3, 2)
+    use_sib(2, 3, 2)
     mul_z(4)
-    sib_copy(1, 4).wait_recv()
-    mul_z(12)
+    use_sib(2, 4, 1)
     z = zacc[...].astype(BF16).astype(F32)
     gate = z / (1.0 + jnp.exp(-z))
 
+    a2a_start(0, lambda k: usrc.at[other(k)], lambda k: urecv.at[k])
     a2a_wait(2, sin.at[pl.ds(0, n_seq)])
     entering = jnp.concatenate(
         [jnp.concatenate([sin[2 * r], sin[2 * r + 1]], axis=1) for r in range(8)], axis=0
     )
-    gated = (ybuf[...] + ecum[...] * dot(c_m, entering)) * gate
+    e_hi, e_lo = split(entering)
+    gated = (ybuf[...] + ecum[...] * (dot(c_m, e_hi) + dot(c_m, e_lo))) * gate
     sq_hi, sq_lo = split(gated * gated)
     same = (iota((CH, CH), 0) // HEAD_DIM == iota((CH, CH), 1) // HEAD_DIM).astype(F32).astype(BF16)
     mean_sq = (dot(sq_hi, same) + dot(sq_lo, same)) * (1.0 / HEAD_DIM)
@@ -502,9 +508,9 @@
     first_half = to_sibling(0, psrc.at[1 - c], psib)
     first_half.start()
     first_half.wait_recv()
-    pall[y] = psrc[c] + psib[...]
-
-    def p_start(k, carry):
+    pall[y] = (psrc[c] + psib[...]).astype(BF16)
+
+    for k in range(RING - 1):
         peer = lax.rem(y + outward(k, RING // 2), RING) * 2 + c
         pltpu.make_async_remote_copy(
             src_ref=pall.at[y],
@@ -514,12 +520,10 @@
             device_id={"seq": peer},
             device_id_type=MESH,
         ).start()
-        return carry
-
-    lax.fori_loop(0, RING - 1, p_start, 0)
+
     most = pall.at[pl.ds(0, RING - 1)]
     pltpu.make_async_copy(most, most, p_recv.at[1]).wait()
-    phalf[c] = jnp.sum(pall[...], axis=0)
+    phalf[c] = jnp.sum(pall[...].astype(F32), axis=0)
     second_half = to_sibling(2, phalf.at[c], phalf.at[c])
     second_half.start()
     second_half.wait_recv()
@@ -532,7 +536,7 @@
         for h in range(NHEAD):
             fsrc[h * NIVF + o] = value[o * 8 : o * 8 + 8, h * 128 : h * 128 + 128]
 
-    def f_start(k, carry):
+    for k in range(n_far):
         h, o = far(k)
         pltpu.make_async_remote_copy(
             src_ref=fsrc.at[h * NIVF + o],
@@ -542,9 +546,6 @@
             device_id={"head": h, "ivf": o},
             device_id_type=MESH,
         ).start()
-        return carry
-
-    lax.fori_loop(0, n_far, f_start, 0)
 
     def sent(d, carry):
         for n in range(5):
@@ -560,21 +561,18 @@
         return carry
 
     def sib_sent(at, carry):
-        @pl.when(at != 4)
-        def _():
-            sib_copy(0, at).wait_send()
-
-        sib_copy(1, at).wait_send()
+        for kind in range(3):
+            sib_copy(kind, at).wait_send()
         return carry
 
     lax.fori_loop(0, 4, sent, 0)
     lax.fori_loop(0, 8, sib_sent, 0)
-    sib_copy(0, 4, 0).wait_send()
-    sib_copy(0, 4, 1).wait_send()
-    pltpu.make_async_copy(bcbuf.at[pl.ds(0, SHARE - 1)], bcbuf.at[pl.ds(0, SHARE - 1)], bc_send).wait()
+    bc_wait(0, bc_send)
+    bc_wait(1, bc_send)
     a2a_sent(0, urecv)
     a2a_sent(1, srecv.at[pl.ds(0, n_seq)])
     a2a_sent(2, sin.at[pl.ds(0, n_seq)])
+    a2a_sent(3, drecv.at[pl.ds(0, n_seq)])
     first_half.wait_send()
     second_half.wait_send()
     pltpu.make_async_copy(most, most, p_send.at[1]).wait()
@@ -599,17 +597,23 @@
     return pl.pallas_call(
         kernel,
         out_shape=jax.ShapeDtypeStruct((1, CAP, 64), F32),
-        in_specs=[any_spec] * 6 + [vmem_spec] * 6,
+        in_specs=[any_spec] * 12,
         out_specs=vmem_spec,
         scratch_shapes=[
+            vmem((1, SPANS), jnp.int32),
+            vmem((1, SPANS), jnp.int32),
+            vmem((1, LH), F32),
+            vmem((1, LH), F32),
+            vmem((1, LH), F32),
+            vmem((1, CH), F32),
             vmem((TOK, SEQ * KB), BF16),
             vmem((SEQ, AR, CH), BF16),
             vmem((SEQ, KB, CH), BF16),
             vmem((TOK, CH), F32),
             vmem((TOK, CH), F32),
             vmem((BCR + DTR, TOK), F32),
-            vmem((SHARE, BCR, TOK), BF16),
-            vmem((KB, 128), BF16),
+            vmem((2, SHARE, HALF, TOK), BF16),
+            vmem((KB, 2 * STATE), BF16),
             vmem((LH, KB), BF16),
             vmem((CH, 256), BF16),
             vmem((CH, NHEAD * 128), BF16),
@@ -617,10 +621,12 @@
             vmem((SPANS, TOK), F32),
             vmem((SEQ, 8, 128), F32),
             vmem((SEQ - 1, 8, 128), F32),
-            vmem((SEQ, 32, 128), BF16),
-            vmem((SEQ, 32, 128), BF16),
-            vmem((SEQ, 16, 128), BF16),
-            vmem((SEQ, 16, 128), BF16),
+            vmem((2, 8, 128), F32),
+            vmem((SEQ, 8, 128), F32),
+            vmem((SEQ, 16, 128), F32),
+            vmem((SEQ, 16, 128), F32),
+            vmem((SEQ, 16, 128), F32),
+            vmem((SEQ, 16, 128), F32),
             vmem((TOK, TOK), F32),
             vmem((8, TOK), F32),
             vmem((8, TOK), F32),
@@ -628,19 +634,19 @@
             vmem((TOK, CH), F32),
             vmem((2, SPANS, 128), F32),
             vmem((SPANS, 128), F32),
-            vmem((RING, SPANS, 128), F32),
+            vmem((RING, SPANS, 128), BF16),
             vmem((2, SPANS, 128), F32),
             vmem((NHEAD * NIVF, 8, 128), F32),
             vmem((NHEAD * NIVF - 1, 8, 128), F32),
-            dma((6,)),
+            dma((12,)),
             dma((5, 2, 4)),
             dma((5, 8)),
-            dma((4, 8)),
-            dma((4, 8)),
-            dma,
-            dma,
-            dma((3,)),
-            dma((3,)),
+            dma((3, 8)),
+            dma((3, 8)),
+            dma((2,)),
+            dma((2,)),
+            dma((4,)),
+            dma((4,)),
             dma((3,)),
             dma((3,)),
             dma,

time: 76.3 us -> 72.7 us (0.953)
  Pallas kernels: 74.9 us -> 71.3 us
    pallas_call x1, Pallas kernels: 74.9 us -> 71.3 us  [local(): pl.pallas_call(kernel, out_shape=jax.ShapeDtypeStruct((1, CAP, 64), F32),...]
where the time goes in v2:
time: 72.7 us; the launch traced here: 72.5 us
  Pallas kernels  71.3 us (98%)
  local copies, waits for them, and re-layouts  1.26 us (2%)
    pallas_call x1, Pallas kernels, local(): pl.pallas_call(kernel, out_shape=jax.ShapeDtypeStruct((1, CAP, 64), F32),...  71.3 us

profile of v2, /device:TPU:1, one launch (start us, length us, event | category | flops | bytes accessed | tf_op | source)
XLA Modules:
  0.0 72.5 jit_solution(15700417102671158519)
XLA Ops:
  0.0 71.3 %shard_map.118 = f32[1,6,64]{2,1,0:T(8,128)} custom-call(bf16[512,4096]{1,0:T(8,128)(2,1)} %hid_hbm.1, bf16[256,256]{1,0:T(8,128)(2,1)} %wx_hbm.1, bf16[256,256]{1,0:T(8,128)(2,1)} %wz_hbm.1, bf16[4,256]{1,0:T(4,128)(2,1)} %bitcast.7, bf16[256,512]{1,0:T(8,128)(2,1)} %wbc_hbm.1, bf16[256,256]{1,0:T(8,128)(2,1)} %wout_hbm.1, s32[1,32]{1,0:T(1,128)} %bitcast.9, ...), custom_call_target="tpu_custom_call" | custom-call | tf_op jit(solution)/shard_map/pallas_call | solution.py:597
  71.3 1.3 %copy.13 = f32[1,6,64]{2,0,1:T(1,128)} copy(f32[1,6,64]{2,1,0:T(8,128)} %shard_map.118) | data formatting | bytes 3072 | tf_op jit(solution)/shard_map/pallas_call | solution.py:597

commit v3 on v2

--- a/solution.py
+++ b/solution.py
@@ -430,7 +430,7 @@
         cum_row = cumt[pl.ds(h, 1), :]
         dt_row = dtt[pl.ds(h, 1), :]
         for i in range(4):
-            highs, lows = [], []
+            parts = []
             here = slice(i * 128, i * 128 + 128)
             for k in range(i + 1):
                 cols = slice(k * 128, k * 128 + 128)
@@ -438,13 +438,9 @@
                 if k == i:
                     between = jnp.where(iota((128, 128), 0) >= iota((128, 128), 1), between, -1e30)
                 weight = scores[here, cols] * jnp.exp(between) * dt_row[:, cols]
-                high, low = split(weight)
-                highs.append(high)
-                lows.append(low)
-            if i:
-                highs, lows = [jnp.concatenate(highs, axis=1)], [jnp.concatenate(lows, axis=1)]
-            rows = xm[0 : i * 128 + 128, :]
-            ybuf[here, :] += dot(highs[0], rows) + dot(lows[0], rows)
+                parts.append(weight.astype(BF16))
+            block = jnp.concatenate(parts, axis=1) if i else parts[0]
+            ybuf[here, :] += dot(block, xm[0 : i * 128 + 128, :])
         return carry
 
     lax.fori_loop(0, LH, one_head, 0)
@@ -583,7 +579,7 @@
     own = fsrc[head * NIVF + ivf]
     pltpu.make_async_copy(frecv, frecv, f_recv).wait()
     result = (own + jnp.sum(frecv[...], axis=0))[:, 0:64] + mean_u
-    out_ref[0] = result[0:CAP, :]
+    out_ref[:, 0, :] = result[0:CAP, :]
     pltpu.make_async_copy(frecv, frecv, f_send).wait()
 
 
@@ -594,9 +590,9 @@
     vmem_spec = pl.BlockSpec(memory_space=pltpu.VMEM)
     vmem = pltpu.VMEM
     dma = pltpu.SemaphoreType.DMA
-    return pl.pallas_call(
+    rows = pl.pallas_call(
         kernel,
-        out_shape=jax.ShapeDtypeStruct((1, CAP, 64), F32),
+        out_shape=jax.ShapeDtypeStruct((CAP, 1, 64), F32),
         in_specs=[any_spec] * 12,
         out_specs=vmem_spec,
         scratch_shapes=[
@@ -669,6 +665,7 @@
         d_skip.reshape(1, LH),
         norm_gain.reshape(1, CH),
     )
+    return jnp.transpose(rows, (1, 0, 2))
 
 
 def solution(mesh):

time: 72.7 us -> 71.5 us (0.983)
  Pallas kernels: 71.3 us -> 70.1 us
    pallas_call x1 -> x0, local copies, waits for them, and re-layouts: 1.26 us -> none  [local(): pl.pallas_call(kernel, out_shape=jax.ShapeDtypeStruct((1, CAP, 64), F32),...]
    unnamed x0 -> x1, local copies, waits for them, and re-layouts: none -> 1.26 us
    pallas_call x1, Pallas kernels: 71.3 us -> 70.1 us  [local(): pl.pallas_call(kernel, out_shape=jax.ShapeDtypeStruct((CAP, 1, 64), F32),...]
where the time goes in v3:
time: 71.5 us; the launch traced here: 71.4 us
  Pallas kernels  70.1 us (98%)
  local copies, waits for them, and re-layouts  1.26 us (2%)
    pallas_call x1, Pallas kernels, local(): pl.pallas_call(kernel, out_shape=jax.ShapeDtypeStruct((CAP, 1, 64), F32),...  70.1 us

profile of v3, /device:TPU:1, one launch (start us, length us, event | category | flops | bytes accessed | tf_op | source)
XLA Modules:
  0.0 71.4 jit_solution(5188547770819043442)
XLA Ops:
  0.0 70.1 %shard_map.118 = f32[6,1,64]{2,1,0:T(1,128)} custom-call(bf16[512,4096]{1,0:T(8,128)(2,1)} %hid_hbm.1, bf16[256,256]{1,0:T(8,128)(2,1)} %wx_hbm.1, bf16[256,256]{1,0:T(8,128)(2,1)} %wz_hbm.1, bf16[4,256]{1,0:T(4,128)(2,1)} %bitcast.9, bf16[256,512]{1,0:T(8,128)(2,1)} %wbc_hbm.1, bf16[256,256]{1,0:T(8,128)(2,1)} %wout_hbm.1, s32[1,32]{1,0:T(1,128)} %bitcast.11, ...), custom_call_target="tpu_custom_call" | custom-call | tf_op jit(solution)/shard_map/pallas_call | solution.py:593
  70.1 1.3 %copy.14 = f32[1,6,64]{2,0,1:T(1,128)} copy(f32[1,6,64]{2,0,1:T(1,128)} %bitcast.8) | data formatting | bytes 3072

commit v4 on v3

--- a/solution.py
+++ b/solution.py
@@ -329,15 +329,10 @@
         sib_copy(0, d).start()
         sib_copy(0, 4 + d).start()
 
-        @pl.when(d == 2)
+        @pl.when(d == 3)
         def _():
             z_start(3)
             z_start(4)
-
-        @pl.when(d == 3)
-        def _():
-            z_step(3, 1)
-            z_step(4, 1)
 
         return carry
 
@@ -394,8 +389,8 @@
     ring_wait(1, 4)
     ring_wait(2, 4)
     sib_copy(0, 4).start()
-    z_step(3, 2)
-    z_step(4, 2)
+    z_step(3, 1)
+    z_step(4, 1)
     sib_copy(2, 0).start()
     mul_x(4)
 
@@ -416,8 +411,8 @@
 
     for j in (2, 1, 3):
         bc_copy(1, j).start()
-    z_step(3, 3)
-    z_step(4, 3)
+    z_step(3, 2)
+    z_step(4, 2)
     bc_wait(1, bc_recv)
     c_m = bcbuf[1].reshape(STATE, TOK).astype(F32).T.astype(BF16)
     scores[...] = dot(c_m, b_t)
@@ -454,6 +449,8 @@
     lax.fori_loop(0, SEQ, enter, jnp.zeros((16, 128), F32))
     a2a_start(2, lambda k: sout.at[other(k)], lambda k: sin.at[seq])
     sin[seq] = sout[seq]
+    z_step(3, 3)
+    z_step(4, 3)
     mul_z(0)
     use_sib(2, 0, 1)
     use_mine(2, 1, 2)
@@ -483,9 +480,9 @@
     )
     e_hi, e_lo = split(entering)
     gated = (ybuf[...] + ecum[...] * (dot(c_m, e_hi) + dot(c_m, e_lo))) * gate
-    sq_hi, sq_lo = split(gated * gated)
+    square = (gated * gated).astype(BF16)
     same = (iota((CH, CH), 0) // HEAD_DIM == iota((CH, CH), 1) // HEAD_DIM).astype(F32).astype(BF16)
-    mean_sq = (dot(sq_hi, same) + dot(sq_lo, same)) * (1.0 / HEAD_DIM)
+    mean_sq = dot(square, same) * (1.0 / HEAD_DIM)
     normed = (gated * lax.rsqrt(mean_sq + 1e-05) * gain_ref[...]).astype(BF16)
     pooled = dot(ins[...].astype(BF16), normed) * span_inv
     psrc[0] = pooled[:, 0:128]

time: 71.5 us -> 70.7 us (0.989)
  Pallas kernels: 70.1 us -> 69.3 us
    pallas_call x1, Pallas kernels: 70.1 us -> 69.3 us  [local(): pl.pallas_call(kernel, out_shape=jax.ShapeDtypeStruct((CAP, 1, 64), F32),...]
where the time goes in v4:
time: 70.7 us; the launch traced here: 70.6 us
  Pallas kernels  69.3 us (98%)
  local copies, waits for them, and re-layouts  1.26 us (2%)
    pallas_call x1, Pallas kernels, local(): pl.pallas_call(kernel, out_shape=jax.ShapeDtypeStruct((CAP, 1, 64), F32),...  69.3 us

profile of v4, /device:TPU:1, one launch (start us, length us, event | category | flops | bytes accessed | tf_op | source)
XLA Modules:
  0.0 70.6 jit_solution(8310741207103989581)
XLA Ops:
  0.0 69.3 %shard_map.118 = f32[6,1,64]{2,1,0:T(1,128)} custom-call(bf16[512,4096]{1,0:T(8,128)(2,1)} %hid_hbm.1, bf16[256,256]{1,0:T(8,128)(2,1)} %wx_hbm.1, bf16[256,256]{1,0:T(8,128)(2,1)} %wz_hbm.1, bf16[4,256]{1,0:T(4,128)(2,1)} %bitcast.9, bf16[256,512]{1,0:T(8,128)(2,1)} %wbc_hbm.1, bf16[256,256]{1,0:T(8,128)(2,1)} %wout_hbm.1, s32[1,32]{1,0:T(1,128)} %bitcast.11, ...), custom_call_target="tpu_custom_call" | custom-call | tf_op jit(solution)/shard_map/pallas_call | solution.py:590
  69.3 1.3 %copy.14 = f32[1,6,64]{2,0,1:T(1,128)} copy(f32[1,6,64]{2,0,1:T(1,128)} %bitcast.8) | data formatting | bytes 3072

commit v5 on v4

--- a/solution.py
+++ b/solution.py
@@ -377,7 +377,6 @@
     dtt[...] = step_size
     spread = (iota((8, CH), 1) // HEAD_DIM == iota((8, CH), 0)).astype(F32)
     tail = dot(jnp.exp(total - cum) * step_size, spread, TN, HIGHEST)
-    ecum[...] = dot(jnp.exp(cum), spread, TN, HIGHEST)
     total_row = jnp.sum(total * spread, axis=0, keepdims=True)
     skip_row = jnp.sum(skip * spread, axis=0, keepdims=True)
     for half in (0, 1):
@@ -417,6 +416,7 @@
     c_m = bcbuf[1].reshape(STATE, TOK).astype(F32).T.astype(BF16)
     scores[...] = dot(c_m, b_t)
     ybuf[...] = x_f * skip_row
+    ecum[...] = dot(jnp.exp(cum), spread, TN, HIGHEST)
 
     def one_head(h, carry):
         pick = (iota((8, 128), 0) == h).astype(F32)

time: 70.7 us -> 71.3 us (level)
  no operation moved by 1% of the time
where the time goes in v5:
time: 71.3 us; the launch traced here: 71.1 us
  Pallas kernels  69.8 us (98%)
  local copies, waits for them, and re-layouts  1.26 us (2%)
    pallas_call x1, Pallas kernels, local(): pl.pallas_call(kernel, out_shape=jax.ShapeDtypeStruct((CAP, 1, 64), F32),...  69.8 us

profile of v5, /device:TPU:1, one launch (start us, length us, event | category | flops | bytes accessed | tf_op | source)
XLA Modules:
  0.0 71.1 jit_solution(6266975730747287423)
XLA Ops:
  0.0 69.8 %shard_map.118 = f32[6,1,64]{2,1,0:T(1,128)} custom-call(bf16[512,4096]{1,0:T(8,128)(2,1)} %hid_hbm.1, bf16[256,256]{1,0:T(8,128)(2,1)} %wx_hbm.1, bf16[256,256]{1,0:T(8,128)(2,1)} %wz_hbm.1, bf16[4,256]{1,0:T(4,128)(2,1)} %bitcast.9, bf16[256,512]{1,0:T(8,128)(2,1)} %wbc_hbm.1, bf16[256,256]{1,0:T(8,128)(2,1)} %wout_hbm.1, s32[1,32]{1,0:T(1,128)} %bitcast.11, ...), custom_call_target="tpu_custom_call" | custom-call | tf_op jit(solution)/shard_map/pallas_call | solution.py:590
  69.8 1.3 %copy.14 = f32[1,6,64]{2,0,1:T(1,128)} copy(f32[1,6,64]{2,0,1:T(1,128)} %bitcast.8) | data formatting | bytes 3072
